TPU v7x, 256 devices: a whole 4x4x8 slice. The times are simulated.
256 devices in a mesh: azi: 8 (over y, core), rad: 16 (over x, z_lo), axl: 2 (over z_hi).
Axes of the slice: x: 4, y: 4, z: 8 (z_hi: 2, z_lo: 4; z = z_hi * 4 + z_lo), core: 2. Of those that a mesh axis runs over, the one named last changes fastest.
Arguments:
- perturbation: float32 [5, 8, 1024, 2048], P(None, 'axl', 'rad', 'azi'), may hold values from -6 to 6
- axial_velocity: float32 [8, 1024], P('axl', 'rad'), may hold values from 0.4 to 1.2
- swirl_velocity: float32 [8, 1024], P('axl', 'rad'), may hold values from -0.8 to 0.8
- sound_speed: float32 [8, 1024], P('axl', 'rad'), may hold values from 1 to 1.6
- rotor_offset: int32 [1], replicated, may hold values from 0 to 2047
Outputs:
- tendency: float32 [5, 8, 1024, 2048], P(None, 'axl', 'rad', 'azi')
All inputs are finite; a program needn't handle non-finite values.
Results may differ from a plain program's by a relative error of at most 0.000065.
Values sent between devices are 32-bit elements; how exact they have to be, the bound alone decides.
No kernel may reach another device: no remote copies, remote signals or barrier semaphores. Data moves between devices by JAX's collectives and lax.ppermute only.
A program may use at most 128 MiB of HBM per device.

v0:
```python
import jax
import jax.numpy as jnp
import numpy as np
from jax import lax
from jax.sharding import PartitionSpec as P

NA = 2048
BAND = 128
WEIGHTS = (45.0 / 60.0, -9.0 / 60.0, 1.0 / 60.0)


def partner(value, axis, distance):
    mask = 2**distance
    pairs = [(source, source ^ mask) for source in range(lax.axis_size(axis))]
    return lax.ppermute(value, axis, pairs)


def with_halo(block, sides, width):
    for axis, dim in sides:
        count = lax.axis_size(axis)
        forward = [(i, i + 1) for i in range(count - 1)]
        backward = [(target, source) for source, target in forward]
        low = lax.ppermute(
            lax.slice_in_dim(block, block.shape[dim] - width, None, axis=dim), axis, forward
        )
        high = lax.ppermute(lax.slice_in_dim(block, 0, width, axis=dim), axis, backward)
        block = jnp.concatenate([low, block, high], axis=dim)
    return block


def stencil_coefs(cells, reach):
    offsets = np.arange(1, reach + 1)
    signs = np.where(offsets % 2 == 1, 1.0, -1.0)
    angles = np.pi * offsets / cells
    values = np.pi / cells * signs * np.cos(angles) / np.sin(angles)
    return np.concatenate([np.zeros(1), values])


def signed_table(coefs, offsets):
    reach = coefs.shape[0] - 1
    magnitude = np.abs(offsets)
    picked = coefs[np.minimum(magnitude, reach)]
    return np.where(magnitude <= reach, np.sign(offsets) * picked, 0.0)


def band_table(coefs, columns):
    reach = coefs.shape[0] - 1
    source = np.arange(columns + 2 * reach)
    target = np.arange(columns)
    offsets = source[:, None] - target[None, :] - reach
    return signed_table(coefs, offsets)


def central_diff(padded, axis_pos):
    extent = padded.shape[axis_pos] - 6
    result = jnp.zeros_like(lax.slice_in_dim(padded, 3, 3 + extent, axis=axis_pos))
    for reach_k, weight in enumerate(WEIGHTS, start=1):
        upper = lax.slice_in_dim(padded, 3 + reach_k, 3 + reach_k + extent, axis=axis_pos)
        lower = lax.slice_in_dim(padded, 3 - reach_k, 3 - reach_k + extent, axis=axis_pos)
        result = result + weight * (upper - lower)
    return result


def section_terms(padded, angular, axial_vel, swirl_vel, sound_vel, metric):
    deriv_x = central_diff(padded, 1)
    stream = axial_vel[:, :, None]
    turning = (swirl_vel * metric[None, :])[:, :, None]
    speed_sq = (sound_vel * sound_vel)[:, :, None]
    scale = metric[:, None]
    convect = stream * deriv_x + turning * angular
    spread = deriv_x[1] + scale * angular[3]
    return jnp.stack(
        [
            -(convect[0] + spread),
            -(convect[1] + deriv_x[4]),
            -convect[2],
            -(convect[3] + scale * angular[4]),
            -(convect[4] + speed_sq * spread),
        ]
    )


def radial_terms(radial, sound_vel):
    speed_sq = (sound_vel * sound_vel)[:, :, None]
    blank = jnp.zeros_like(radial[0])
    return jnp.stack([-radial[0], blank, -radial[1], blank, -speed_sq * radial[0]])


def make_metric(first_row, row_count, radial_total):
    index = (first_row + jnp.arange(row_count, dtype=jnp.int32)).astype(jnp.float32)
    return 2.0 / (1.0 + (index + 0.5) / radial_total)


def rotate_edge(edge_lines, start_cell):
    doubled = jnp.concatenate([edge_lines, edge_lines], axis=3)
    return lax.dynamic_slice_in_dim(doubled, start_cell, NA, 3)


def attach_planes(values, received, stator_side):
    blanks = jnp.zeros_like(received)
    lower = jnp.where(stator_side, blanks, received)
    upper = jnp.where(stator_side, received, blanks)
    return jnp.concatenate([lower, values, upper], axis=1)


def tiled_lines(lines_all, coefs):
    width = BAND
    blocks = NA // width
    lead = lines_all.shape[:3]
    tiles = lines_all.reshape(lead + (blocks, width))
    banded = band_table(coefs, width)
    left_part = jnp.asarray(banded[0:width], dtype=jnp.float32)
    middle_part = jnp.asarray(banded[width : 2 * width], dtype=jnp.float32)
    right_part = jnp.asarray(banded[2 * width : 3 * width], dtype=jnp.float32)
    form = "fxrke,ej->fxrkj"
    middle = jnp.einsum(
        form,
        tiles,
        middle_part,
        precision=lax.Precision.HIGHEST,
        preferred_element_type=jnp.float32,
    )
    from_left = jnp.einsum(
        form, tiles, left_part, precision=lax.Precision.HIGHEST, preferred_element_type=jnp.float32
    )
    from_right = jnp.einsum(
        form, tiles, right_part, precision=lax.Precision.HIGHEST, preferred_element_type=jnp.float32
    )
    result = middle + jnp.roll(from_left, 1, axis=3) + jnp.roll(from_right, -1, axis=3)
    return result.reshape(lines_all.shape)


def per_device(perturbation, axial_velocity, swirl_velocity, sound_speed, rotor_offset):
    azi_count = lax.axis_size("azi")
    rad_count = lax.axis_size("rad")
    rows = perturbation.shape[2]
    sub_rows = rows // azi_count
    azi_pos = lax.axis_index("azi")
    rad_pos = lax.axis_index("rad")
    axl_pos = lax.axis_index("axl")
    radial_total = rows * rad_count
    coefs = stencil_coefs(NA, BAND)
    shift_cells = rotor_offset[0]
    stator_side = axl_pos == 0
    start_cell = jnp.where(stator_side, shift_cells, NA - shift_cells) % NA
    lines_all = lax.all_to_all(perturbation, "azi", split_axis=2, concat_axis=3, tiled=True)
    angular = tiled_lines(lines_all, coefs)
    edge_lines = jnp.where(stator_side, lines_all[:, -3:], lines_all[:, :3])
    received = partner(rotate_edge(edge_lines, start_cell), "axl", 0)
    padded = attach_planes(lines_all, received, stator_side)
    row_start = azi_pos * sub_rows
    axial_sub = lax.dynamic_slice_in_dim(axial_velocity, row_start, sub_rows, 1)
    swirl_sub = lax.dynamic_slice_in_dim(swirl_velocity, row_start, sub_rows, 1)
    sound_sub = lax.dynamic_slice_in_dim(sound_speed, row_start, sub_rows, 1)
    metric = make_metric(rad_pos * rows + row_start, sub_rows, radial_total)
    partial_lines = section_terms(padded, angular, axial_sub, swirl_sub, sound_sub, metric)
    partial_value = lax.all_to_all(partial_lines, "azi", split_axis=3, concat_axis=2, tiled=True)
    pair = jnp.stack([perturbation[2], perturbation[4]])
    pair_pad = with_halo(pair, (("rad", 2),), 3)
    radial = central_diff(pair_pad, 2)
    return partial_value + radial_terms(radial, sound_speed)


def solution(mesh):
    return jax.shard_map(
        per_device,
        mesh=mesh,
        in_specs=(
            P(None, "axl", "rad", "azi"),
            P("axl", "rad"),
            P("axl", "rad"),
            P("axl", "rad"),
            P(),
        ),
        out_specs=P(None, "axl", "rad", "azi"),
        check_vma=False,
    )
```

profile of v0, /device:TPU:1, one launch (start us, length us, event | category | flops | bytes accessed | tf_op | source)
XLA Modules:
  0.0 211.9 jit_solution(11327305505855242520)
XLA Ops:
  0.0 3.5 %copy.17 = f32[5,4,64,256]{3,0,1,2:T(8,128)} copy(f32[5,4,64,256]{3,2,1,0:T(8,128)} %param.8) | data formatting | bytes 2621440 | tf_op args[0]
  3.5 6.7 %all-to-all-start = ((f32[5,4,64,256]{3,0,1,2:T(8,128)}), f32[5,4,64,256]{3,0,1,2:T(8,128)S(1)}, u32[]{:S(2)}, u32[]{:S(2)}) async-start(f32[5,4,64,256]{3,0,1,2:T(8,128)} %copy.17), calls=%async_computation | async-start | bytes 4194304 | tf_op jit(solution)/shard_map/all_to_all | solution.py:146
  10.2 0.0 copy-start.7
  10.2 0.0 copy-start.8
  10.2 0.0 copy-start.9
  10.2 1.1 fusion.32
  11.4 1.3 collective-permute-start.1
  12.7 4.0 %collective-permute-start.2 = (f32[2,4,3,256]{3,2,1,0:T(4,128)S(1)}, f32[2,4,3,256]{3,2,1,0:T(4,128)S(1)}, u32[]{:S(2)}, u32[]{:S(2)}) collective-permute-start(f32[2,4,3,256]{3,2,1,0:T(4,128)S(1)} %get-tuple-element.16), channel_id=1, source_target_pairs={{0,2},{2,4},{4,6},{6,8},{8,10},{10,12},{12,14},{14,16},{16,18},{18... | collective-permute-start | bytes 73736 | tf_op jit(solution)/shard_map/ppermute | solution.py:23
  16.7 0.0 copy-done.7
  16.7 0.0 copy-done.8
  16.7 0.0 copy-done.9
  16.7 0.1 dynamic-slice_multiply_fusion.1
  16.8 0.1 dynamic-slice_multiply_fusion
  17.6 0.0 collective-permute-done.1
  17.6 0.1 collective-permute-done.2
  17.7 0.9 pad_maximum_fusion.2
  18.6 18.0 %all-to-all-done = f32[5,4,64,256]{3,0,1,2:T(8,128)S(1)} async-done(((f32[5,4,64,256]{3,0,1,2:T(8,128)}), f32[5,4,64,256]{3,0,1,2:T(8,128)S(1)}, u32[]{:S(2)}, u32[]{:S(2)}) %all-to-all-start) | async-done | bytes 1310752 | tf_op jit(solution)/shard_map/all_to_all | solution.py:146
  36.6 1.3 copy-done.1
  37.9 2.4 %copy.25 = f32[5,4,8,8,256]{4,2,3,1,0:T(8,128)S(1)} copy(f32[5,4,8,8,256]{4,0,1,3,2:T(8,128)} %bitcast.54) | data formatting | bytes 2621440 | tf_op jit(solution)/shard_map/all_to_all | solution.py:146
  40.2 0.0 copy-start
  40.3 1.0 copy-done
  41.3 0.2 all_to_all.29
  41.5 1.4 reshape.55
  42.9 0.1 slice_select_fusion
  43.0 0.0 copy-start.6
  43.0 1.6 fusion.14
  44.5 6.1 %collective-permute-start = (f32[5,3,8,2048]{3,2,1,0:T(8,128)}, f32[5,3,8,2048]{3,2,1,0:T(8,128)}, u32[]{:S(2)}, u32[]{:S(2)}) collective-permute-start(f32[5,3,8,2048]{3,2,1,0:T(8,128)} %fusion.14), channel_id=1, source_target_pairs={{0,1},{1,0},{2,3},{3,2},{4,5},{5,4},{6,7},{7,6},{8,9},{9,8},{10,11... | collective-permute-start | bytes 2949128 | tf_op jit(solution)/shard_map/ppermute | solution.py:15
  50.7 0.0 copy-done.6
  50.7 1.2 convolution_bitcast_fusion
  51.8 0.0 copy-start.5
  51.9 0.1 slice.163
  52.1 0.6 copy-done.5
  52.7 1.2 convolution_bitcast_fusion.1
  53.9 0.1 slice.161
  54.0 0.0 copy-done.4
  54.0 2.5 %fusion.1 = f32[5,4,8,16,128]{4,3,2,1,0:T(8,128)} fusion(f32[128,128,1,1,1]{1,0,4,3,2:T(8,128)S(1)} %copy-done.4, f32[5,4,8,16,128]{4,3,2,1,0:T(8,128)S(1)} %reshape.55, f32[5,4,8,15,128]{4,3,2,1,0:T(8,128)S(1)} %bitcast.55, f32[5,4,8,1,128]{4,3,2,1,0:T(1,128)S(1)} %slice.161, f32[5,4,8,1,128]{4,3,2,1,0:T(1,128)S(1)} %slice.164, ...), kind=kOutput, calls=%fused_computation.14 | convolution fusion | flops 504627200 | bytes 5308416 | tf_op jit(solution)/shard_map/fxrke,ej->fxrkj/dot_general | solution.py:116
  56.5 1.5 reshape.56
  58.0 1.9 fusion.31
  59.9 1.0 squeeze.7
  60.9 1.7 squeeze.8
  62.6 14.3 %collective-permute-done = f32[5,3,8,2048]{3,2,1,0:T(8,128)} collective-permute-done((f32[5,3,8,2048]{3,2,1,0:T(8,128)}, f32[5,3,8,2048]{3,2,1,0:T(8,128)}, u32[]{:S(2)}, u32[]{:S(2)}) %collective-permute-start) | collective-permute-done | bytes 983072 | tf_op jit(solution)/shard_map/ppermute | solution.py:15
  76.9 1.4 broadcast_select_fusion.1
  78.3 1.1 multiply_add_fusion
  79.4 0.0 copy-start.3
  79.4 0.1 fusion.29
  79.6 0.7 copy-done.3
  80.4 0.1 fusion.24
  80.5 0.1 fusion.22
  80.6 12.5 %copy.19 = f32[5,4,8,2048]{2,1,0,3:T(4,128)} copy(f32[5,4,8,2048]{3,2,1,0:T(8,128)S(1)} %fusion.22) | data formatting | bytes 2621440 | tf_op jit(solution)/shard_map/stack | solution.py:72
  93.1 26.6 %reshape.60 = f32[8,1,40960]{2,1,0:T(1,128)} reshape(f32[2048,5,4,8]{3,2,1,0:T(4,128)} %bitcast.50) | data formatting | bytes 2621440
  119.8 20.2 %all-to-all-start.1 = ((f32[8,1,40960]{2,1,0:T(1,128)}), f32[8,1,40960]{2,1,0:T(1,128)S(1)}, u32[]{:S(2)}, u32[]{:S(2)}) async-start(f32[8,1,40960]{2,1,0:T(1,128)} %reshape.60), calls=%async_computation.1 | async-start | bytes 2621440 | tf_op jit(solution)/shard_map/all_to_all | solution.py:157
  140.0 0.0 copy-done.2
  140.0 0.3 fusion.16
  140.3 0.7 negate_dynamic-update-slice_fusion
  141.0 0.7 broadcast_dynamic-update-slice_fusion
  141.8 0.7 fusion.20
  142.5 0.7 broadcast_dynamic-update-slice_fusion.1
  143.2 0.8 multiply_dynamic-update-slice_fusion
  144.0 13.9 %all-to-all-done.1 = f32[8,1,40960]{2,1,0:T(1,128)S(1)} async-done(((f32[8,1,40960]{2,1,0:T(1,128)}), f32[8,1,40960]{2,1,0:T(1,128)S(1)}, u32[]{:S(2)}, u32[]{:S(2)}) %all-to-all-start.1) | async-done | bytes 1310752 | tf_op jit(solution)/shard_map/all_to_all | solution.py:157
  157.9 0.5 broadcast.89
  158.4 3.7 %reduce = f32[8,40960]{1,0:T(8,128)S(1)} reduce(f32[8,1,40960]{2,1,0:T(1,128)S(1)} %all-to-all-done.1, f32[]{:T(128)} %broadcast.89), dimensions={1}, to_apply=%all_to_all.30.reduce_sub_computation | reduce | bytes 2621444 | tf_op jit(solution)/shard_map/all_to_all | solution.py:157
  162.2 32.6 %reshape.61 = f32[2048,5,4,8]{3,2,1,0:T(4,128)} reshape(f32[8,40960]{1,0:T(8,128)S(1)} %reduce) | data formatting | bytes 2621440
  194.8 14.5 %copy.20 = f32[5,4,8,8,256]{4,3,2,1,0:T(8,128)S(1)} copy(f32[5,4,8,8,256]{3,1,0,4,2:T(4,128)} %bitcast.51) | data formatting | bytes 2621440 | tf_op jit(solution)/shard_map/all_to_all | solution.py:157
  209.4 2.6 %bitcast_add_fusion = f32[5,4,64,256]{3,2,1,0:T(8,128)} fusion(f32[5,4,64,256]{3,2,1,0:T(8,128)} %multiply_dynamic-update-slice_fusion, f32[5,4,8,8,256]{4,3,2,1,0:T(8,128)S(1)} %copy.20), kind=kLoop, calls=%fused_computation.29 | loop fusion | flops 327680 | bytes 3932160 | tf_op jit(solution)/shard_map/add | solution.py:161
  (9 shorter events, 0.1 us)
Async XLA Ops:
  3.5 33.1 %all-to-all-start = ((f32[5,4,64,256]{3,0,1,2:T(8,128)}), f32[5,4,64,256]{3,0,1,2:T(8,128)S(1)}, u32[]{:S(2)}, u32[]{:S(2)}) async-start(f32[5,4,64,256]{3,0,1,2:T(8,128)} %copy.17), calls=%async_computation | async-start | bytes 4194304 | tf_op jit(solution)/shard_map/all_to_all | solution.py:146
  10.2 6.5 %copy-start.7 = (f32[4,64]{1,0:T(4,128)S(1)}, f32[4,64]{1,0:T(4,128)}, u32[]{:S(2)}) copy-start(f32[4,64]{1,0:T(4,128)} %param.11) | copy-start | bytes 3076
  10.2 6.5 %copy-start.8 = (f32[4,64]{1,0:T(4,128)S(1)}, f32[4,64]{1,0:T(4,128)}, u32[]{:S(2)}) copy-start(f32[4,64]{1,0:T(4,128)} %param.10) | copy-start | bytes 3076
  10.2 6.5 %copy-start.9 = (f32[4,64]{1,0:T(4,128)S(1)}, f32[4,64]{1,0:T(4,128)}, u32[]{:S(2)}) copy-start(f32[4,64]{1,0:T(4,128)} %param.9) | copy-start | bytes 3076
  11.4 6.2 %collective-permute-start.1 = (f32[2,4,3,256]{3,2,1,0:T(4,128)S(1)}, f32[2,4,3,256]{3,2,1,0:T(4,128)S(1)}, u32[]{:S(2)}, u32[]{:S(2)}) collective-permute-start(f32[2,4,3,256]{3,2,1,0:T(4,128)S(1)} %get-tuple-element.15), channel_id=1, source_target_pairs={{2,0},{4,2},{6,4},{8,6},{10,8},{12,10},{14,12},{16,14},{18,16},{20... | collective-permute-start | bytes 73736 | tf_op jit(solution)/shard_map/ppermute | solution.py:26
  12.7 5.0 %collective-permute-start.2 = (f32[2,4,3,256]{3,2,1,0:T(4,128)S(1)}, f32[2,4,3,256]{3,2,1,0:T(4,128)S(1)}, u32[]{:S(2)}, u32[]{:S(2)}) collective-permute-start(f32[2,4,3,256]{3,2,1,0:T(4,128)S(1)} %get-tuple-element.16), channel_id=1, source_target_pairs={{0,2},{2,4},{4,6},{6,8},{8,10},{10,12},{12,14},{14,16},{16,18},{18... | collective-permute-start | bytes 73736 | tf_op jit(solution)/shard_map/ppermute | solution.py:23
  36.6 1.3 copy-start.1
  40.2 1.1 copy-start
  43.0 7.7 %copy-start.6 = (f32[128,128,1,1,1]{1,0,4,3,2:T(8,128)S(1)}, f32[128,128,1,1,1]{1,0,4,3,2:T(8,128)}, u32[]{:S(2)}) copy-start(f32[128,128,1,1,1]{1,0,4,3,2:T(8,128)} %constant.66) | copy-start | bytes 196612
  44.5 32.3 %collective-permute-start = (f32[5,3,8,2048]{3,2,1,0:T(8,128)}, f32[5,3,8,2048]{3,2,1,0:T(8,128)}, u32[]{:S(2)}, u32[]{:S(2)}) collective-permute-start(f32[5,3,8,2048]{3,2,1,0:T(8,128)} %fusion.14), channel_id=1, source_target_pairs={{0,1},{1,0},{2,3},{3,2},{4,5},{5,4},{6,7},{7,6},{8,9},{9,8},{10,11... | collective-permute-start | bytes 2949128 | tf_op jit(solution)/shard_map/ppermute | solution.py:15
  51.8 0.8 copy-start.5
  52.7 1.3 copy-start.4
  79.4 1.0 copy-start.3
  119.8 20.2 %copy-start.2 = (f32[2,4,67,256]{3,2,1,0:T(8,128)S(1)}, f32[2,4,67,256]{3,2,1,0:T(8,128)}, u32[]{:S(2)}) copy-start(f32[2,4,67,256]{3,2,1,0:T(8,128)} %get-tuple-element.14) | copy-start | bytes 1646596
  119.8 38.1 %all-to-all-start.1 = ((f32[8,1,40960]{2,1,0:T(1,128)}), f32[8,1,40960]{2,1,0:T(1,128)S(1)}, u32[]{:S(2)}, u32[]{:S(2)}) async-start(f32[8,1,40960]{2,1,0:T(1,128)} %reshape.60), calls=%async_computation.1 | async-start | bytes 2621440 | tf_op jit(solution)/shard_map/all_to_all | solution.py:157
where the time goes:
time: 213 us; the launch traced here: 212 us
  local copies, waits for them, and re-layouts  107 us (50%)
  waiting for transfers between devices  46.3 us (22%)
  starting transfers between devices  38.4 us (18%)
  other arithmetic  14.5 us (7%)
  matrix products  4.92 us (2%)
    unnamed x25, local copies, waits for them, and re-layouts  68 us
    all_to_all x1, starting transfers between devices, per_device(): lax.all_to_all(partial_lines, 'azi', split_axis=3, concat_axis=2, tiled=T...  20.2 us
    all_to_all x1, waiting for transfers between devices, per_device(): lax.all_to_all(perturbation, 'azi', split_axis=2, concat_axis=3, tiled=True)  18 us
    all_to_all x2, local copies, waits for them, and re-layouts, per_device(): lax.all_to_all(partial_lines, 'azi', split_axis=3, concat_axis=2, tiled=T...  15.1 us
    ppermute x1, waiting for transfers between devices, partner(): return lax.ppermute(value, axis, pairs)  14.3 us
    all_to_all x1, waiting for transfers between devices, per_device(): lax.all_to_all(partial_lines, 'azi', split_axis=3, concat_axis=2, tiled=T...  13.9 us
    another operation x1, local copies, waits for them, and re-layouts, section_terms(): jnp.stack([-(convect[0] + spread), -(convect[1] + deriv_x[4]), -convect[2...  12.5 us
    all_to_all x1, starting transfers between devices, per_device(): lax.all_to_all(perturbation, 'azi', split_axis=2, concat_axis=3, tiled=True)  6.74 us
  transfers between devices with their start and end apart: 5, of which 4 were waited for; matrix products, arithmetic and copies ran while one was open for 8% of the time, Pallas kernels for 0%

commit v1 on v0

--- a/solution.py
+++ b/solution.py
@@ -143,7 +143,15 @@
     shift_cells = rotor_offset[0]
     stator_side = axl_pos == 0
     start_cell = jnp.where(stator_side, shift_cells, NA - shift_cells) % NA
-    lines_all = lax.all_to_all(perturbation, "azi", split_axis=2, concat_axis=3, tiled=True)
+    lines_all = jnp.concatenate(
+        jax.lax.all_to_all(
+            jnp.stack(jnp.split(perturbation, jax.lax.psum(1, axis_name="azi"), axis=2)),
+            concat_axis=0,
+            split_axis=0,
+            axis_name="azi",
+        ),
+        axis=3,
+    )
     angular = tiled_lines(lines_all, coefs)
     edge_lines = jnp.where(stator_side, lines_all[:, -3:], lines_all[:, :3])
     received = partner(rotate_edge(edge_lines, start_cell), "axl", 0)

time: 213 us -> 205 us (0.962)
  waiting for transfers between devices: 46.3 us -> 35.8 us
    all_to_all x1, waiting for transfers between devices: 18 us -> 10.6 us  [per_device(): jax.lax.all_to_all(jnp.stack(jnp.split(perturbation, jax.lax.psum(1, axis...]
    unnamed x25 -> x29, local copies, waits for them, and re-layouts: 68 us -> 71.5 us
    ppermute x1, waiting for transfers between devices: 14.3 us -> 11.1 us  [partner(): return lax.ppermute(value, axis, pairs)]
    all_to_all x2 -> x0, local copies, waits for them, and re-layouts: 2.55 us -> none  [per_device(): lax.all_to_all(perturbation, 'azi', split_axis=2, concat_axis=3, tiled=True)]
  transfers between devices with their start and end apart: 5 -> 5, of which waited for: 4 -> 4; matrix products, arithmetic and copies ran while one was open for 8% -> 10% of each run, Pallas kernels for 0% -> 0%
where the time goes in v1:
time: 205 us; the launch traced here: 204 us
  local copies, waits for them, and re-layouts  109 us (53%)
  starting transfers between devices  38.3 us (19%)
  waiting for transfers between devices  35.8 us (17%)
  other arithmetic  14.5 us (7%)
  matrix products  4.85 us (2%)
    unnamed x29, local copies, waits for them, and re-layouts  71.5 us
    all_to_all x1, starting transfers between devices, per_device(): lax.all_to_all(partial_lines, 'azi', split_axis=3, concat_axis=2, tiled=T...  20.2 us
    all_to_all x2, local copies, waits for them, and re-layouts, per_device(): lax.all_to_all(partial_lines, 'azi', split_axis=3, concat_axis=2, tiled=T...  15.1 us
    all_to_all x1, waiting for transfers between devices, per_device(): lax.all_to_all(partial_lines, 'azi', split_axis=3, concat_axis=2, tiled=T...  13.9 us
    another operation x1, local copies, waits for them, and re-layouts, section_terms(): jnp.stack([-(convect[0] + spread), -(convect[1] + deriv_x[4]), -convect[2...  12.6 us
    ppermute x1, waiting for transfers between devices, partner(): return lax.ppermute(value, axis, pairs)  11.1 us
    all_to_all x1, waiting for transfers between devices, per_device(): jax.lax.all_to_all(jnp.stack(jnp.split(perturbation, jax.lax.psum(1, axis...  10.6 us
    all_to_all x1, starting transfers between devices, per_device(): jax.lax.all_to_all(jnp.stack(jnp.split(perturbation, jax.lax.psum(1, axis...  6.71 us
  transfers between devices with their start and end apart: 5, of which 4 were waited for; matrix products, arithmetic and copies ran while one was open for 10% of the time, Pallas kernels for 0%

profile of v1, /device:TPU:1, one launch (start us, length us, event | category | flops | bytes accessed | tf_op | source)
XLA Modules:
  0.0 203.9 jit_solution(10470136314520981554)
XLA Ops:
  0.0 1.7 bitcast_dynamic-update-slice_fusion.7
  1.7 1.6 bitcast_dynamic-update-slice_fusion.6
  3.3 1.6 bitcast_dynamic-update-slice_fusion.5
  4.9 1.6 bitcast_dynamic-update-slice_fusion.4
  6.5 1.6 bitcast_dynamic-update-slice_fusion.3
  8.1 0.0 copy-done.1
  8.1 0.7 bitcast_dynamic-update-slice_fusion.2
  8.8 0.7 bitcast_dynamic-update-slice_fusion.1
  9.4 0.7 bitcast_dynamic-update-slice_fusion
  10.1 6.7 %all-to-all-start = ((f32[8,5,4,8,256]{4,3,2,1,0:T(8,128)}), f32[8,5,4,8,256]{4,3,2,1,0:T(8,128)S(1)}, u32[]{:S(2)}, u32[]{:S(2)}) async-start(f32[8,5,4,8,256]{4,3,2,1,0:T(8,128)} %bitcast_dynamic-update-slice_fusion), calls=%async_computation | async-start | bytes 2621440 | tf_op jit(solution)/shard_map/all_to_all | solution.py:147
  16.9 1.3 collective-permute-start.1
  18.2 4.0 %collective-permute-start.2 = (f32[2,4,3,256]{3,2,1,0:T(4,128)S(1)}, f32[2,4,3,256]{3,2,1,0:T(4,128)S(1)}, u32[]{:S(2)}, u32[]{:S(2)}) collective-permute-start(f32[2,4,3,256]{3,2,1,0:T(4,128)S(1)} %get-tuple-element.16), channel_id=1, source_target_pairs={{0,2},{2,4},{4,6},{6,8},{8,10},{10,12},{12,14},{14,16},{16,18},{18... | collective-permute-start | bytes 73736 | tf_op jit(solution)/shard_map/ppermute | solution.py:23
  22.2 0.0 copy-done.6
  22.2 0.0 copy-done.7
  22.3 0.0 copy-done.8
  22.3 0.1 dynamic-slice_multiply_fusion.1
  22.3 0.1 dynamic-slice_multiply_fusion
  23.1 0.0 collective-permute-done.1
  23.1 0.1 collective-permute-done.2
  23.2 0.9 pad_maximum_fusion.2
  24.1 10.6 %all-to-all-done = f32[8,5,4,8,256]{4,3,2,1,0:T(8,128)S(1)} async-done(((f32[8,5,4,8,256]{4,3,2,1,0:T(8,128)}), f32[8,5,4,8,256]{4,3,2,1,0:T(8,128)S(1)}, u32[]{:S(2)}, u32[]{:S(2)}) %all-to-all-start) | async-done | bytes 1310752 | tf_op jit(solution)/shard_map/all_to_all | solution.py:147
  34.8 0.1 copy.19
  34.9 0.1 slice_select_fusion
  35.0 1.5 fusion.13
  36.6 6.1 %collective-permute-start = (f32[5,3,8,2048]{3,2,1,0:T(8,128)}, f32[5,3,8,2048]{3,2,1,0:T(8,128)}, u32[]{:S(2)}, u32[]{:S(2)}) collective-permute-start(f32[5,3,8,2048]{3,2,1,0:T(8,128)} %fusion.13), channel_id=1, source_target_pairs={{0,1},{1,0},{2,3},{3,2},{4,5},{5,4},{6,7},{7,6},{8,9},{9,8},{10,11... | collective-permute-start | bytes 2949128 | tf_op jit(solution)/shard_map/ppermute | solution.py:15
  42.7 1.8 copy.12
  44.5 1.4 reshape_reshape.3
  45.9 0.0 copy-done.5
  45.9 1.2 fusion.33
  47.1 0.0 copy-start.4
  47.1 0.1 slice.163
  47.3 0.6 copy-done.4
  47.9 1.2 fusion.32
  49.2 0.1 slice.161
  49.2 0.0 copy-done.3
  49.2 2.5 %fusion = f32[5,4,8,16,128]{4,3,2,1,0:T(8,128)} fusion(f32[5,4,8,16,128]{4,3,2,1,0:T(8,128)S(1)} %reshape_reshape.3, f32[128,128,1,1,1]{1,0,4,3,2:T(8,128)S(1)} %copy-done.3, f32[5,4,8,15,128]{4,3,2,1,0:T(8,128)S(1)} %bitcast.59, f32[5,4,8,1,128]{4,3,2,1,0:T(1,128)S(1)} %slice.161, f32[5,4,8,1,128]{4,3,2,1,0:T(1,128)S(1)} %slice.164, ...), kind=kOutput, calls=%fused_computation.11 | convolution fusion | flops 504627200 | bytes 5308416 | tf_op jit(solution)/shard_map/fxrke,ej->fxrkj/dot_general | solution.py:116
  51.7 1.5 reshape.59
  53.2 1.9 fusion.30
  55.1 1.0 squeeze.7
  56.1 1.7 squeeze.8
  57.8 11.1 %collective-permute-done = f32[5,3,8,2048]{3,2,1,0:T(8,128)} collective-permute-done((f32[5,3,8,2048]{3,2,1,0:T(8,128)}, f32[5,3,8,2048]{3,2,1,0:T(8,128)}, u32[]{:S(2)}, u32[]{:S(2)}) %collective-permute-start) | collective-permute-done | bytes 983072 | tf_op jit(solution)/shard_map/ppermute | solution.py:15
  68.9 1.4 broadcast_select_fusion.1
  70.4 1.1 multiply_add_fusion
  71.5 0.0 copy-start.2
  71.5 0.1 fusion.28
  71.7 0.7 copy-done.2
  72.4 0.1 fusion.23
  72.5 0.1 fusion.21
  72.6 12.6 %copy.14 = f32[5,4,8,2048]{2,1,0,3:T(4,128)} copy(f32[5,4,8,2048]{3,2,1,0:T(8,128)S(1)} %fusion.21) | data formatting | bytes 2621440 | tf_op jit(solution)/shard_map/stack | solution.py:72
  85.2 26.6 %reshape.63 = f32[8,1,40960]{2,1,0:T(1,128)} reshape(f32[2048,5,4,8]{3,2,1,0:T(4,128)} %bitcast.53) | data formatting | bytes 2621440
  111.9 20.2 %all-to-all-start.1 = ((f32[8,1,40960]{2,1,0:T(1,128)}), f32[8,1,40960]{2,1,0:T(1,128)S(1)}, u32[]{:S(2)}, u32[]{:S(2)}) async-start(f32[8,1,40960]{2,1,0:T(1,128)} %reshape.63), calls=%async_computation.1 | async-start | bytes 2621440 | tf_op jit(solution)/shard_map/all_to_all | solution.py:165
  132.1 0.0 copy-done
  132.1 0.3 fusion.15
  132.4 0.7 negate_dynamic-update-slice_fusion
  133.1 0.7 broadcast_dynamic-update-slice_fusion
  133.8 0.7 fusion.19
  134.6 0.7 broadcast_dynamic-update-slice_fusion.1
  135.3 0.8 multiply_dynamic-update-slice_fusion
  136.1 13.9 %all-to-all-done.1 = f32[8,1,40960]{2,1,0:T(1,128)S(1)} async-done(((f32[8,1,40960]{2,1,0:T(1,128)}), f32[8,1,40960]{2,1,0:T(1,128)S(1)}, u32[]{:S(2)}, u32[]{:S(2)}) %all-to-all-start.1) | async-done | bytes 1310752 | tf_op jit(solution)/shard_map/all_to_all | solution.py:165
  150.0 0.5 broadcast.89
  150.5 3.7 %reduce = f32[8,40960]{1,0:T(8,128)S(1)} reduce(f32[8,1,40960]{2,1,0:T(1,128)S(1)} %all-to-all-done.1, f32[]{:T(128)} %broadcast.89), dimensions={1}, to_apply=%all_to_all.17.reduce_sub_computation | reduce | bytes 2621444 | tf_op jit(solution)/shard_map/all_to_all | solution.py:165
  154.2 32.6 %reshape.64 = f32[2048,5,4,8]{3,2,1,0:T(4,128)} reshape(f32[8,40960]{1,0:T(8,128)S(1)} %reduce) | data formatting | bytes 2621440
  186.8 14.5 %copy.15 = f32[5,4,8,8,256]{4,3,2,1,0:T(8,128)S(1)} copy(f32[5,4,8,8,256]{3,1,0,4,2:T(4,128)} %bitcast.54) | data formatting | bytes 2621440 | tf_op jit(solution)/shard_map/all_to_all | solution.py:165
  201.3 2.6 %bitcast_add_fusion = f32[5,4,64,256]{3,2,1,0:T(8,128)} fusion(f32[5,4,64,256]{3,2,1,0:T(8,128)} %multiply_dynamic-update-slice_fusion, f32[5,4,8,8,256]{4,3,2,1,0:T(8,128)S(1)} %copy.15), kind=kLoop, calls=%fused_computation.26 | loop fusion | flops 327680 | bytes 3932160 | tf_op jit(solution)/shard_map/add | solution.py:169
  (14 shorter events, 0.2 us)
Async XLA Ops:
  0.0 8.1 %copy-start.1 = (f32[5,4,64,256]{3,2,1,0:T(8,128)S(1)}, f32[5,4,64,256]{3,2,1,0:T(8,128)}, u32[]{:S(2)}) copy-start(f32[5,4,64,256]{3,2,1,0:T(8,128)} %param.8) | copy-start | bytes 3932164
  10.1 24.6 %all-to-all-start = ((f32[8,5,4,8,256]{4,3,2,1,0:T(8,128)}), f32[8,5,4,8,256]{4,3,2,1,0:T(8,128)S(1)}, u32[]{:S(2)}, u32[]{:S(2)}) async-start(f32[8,5,4,8,256]{4,3,2,1,0:T(8,128)} %bitcast_dynamic-update-slice_fusion), calls=%async_computation | async-start | bytes 2621440 | tf_op jit(solution)/shard_map/all_to_all | solution.py:147
  16.8 5.4 %copy-start.6 = (f32[4,64]{1,0:T(4,128)S(1)}, f32[4,64]{1,0:T(4,128)}, u32[]{:S(2)}) copy-start(f32[4,64]{1,0:T(4,128)} %param.11) | copy-start | bytes 3076
  16.8 5.4 %copy-start.7 = (f32[4,64]{1,0:T(4,128)S(1)}, f32[4,64]{1,0:T(4,128)}, u32[]{:S(2)}) copy-start(f32[4,64]{1,0:T(4,128)} %param.10) | copy-start | bytes 3076
  16.8 5.4 %copy-start.8 = (f32[4,64]{1,0:T(4,128)S(1)}, f32[4,64]{1,0:T(4,128)}, u32[]{:S(2)}) copy-start(f32[4,64]{1,0:T(4,128)} %param.9) | copy-start | bytes 3076
  16.9 6.2 %collective-permute-start.1 = (f32[2,4,3,256]{3,2,1,0:T(4,128)S(1)}, f32[2,4,3,256]{3,2,1,0:T(4,128)S(1)}, u32[]{:S(2)}, u32[]{:S(2)}) collective-permute-start(f32[2,4,3,256]{3,2,1,0:T(4,128)S(1)} %get-tuple-element.15), channel_id=1, source_target_pairs={{2,0},{4,2},{6,4},{8,6},{10,8},{12,10},{14,12},{16,14},{18,16},{20... | collective-permute-start | bytes 73736 | tf_op jit(solution)/shard_map/ppermute | solution.py:26
  18.2 5.0 %collective-permute-start.2 = (f32[2,4,3,256]{3,2,1,0:T(4,128)S(1)}, f32[2,4,3,256]{3,2,1,0:T(4,128)S(1)}, u32[]{:S(2)}, u32[]{:S(2)}) collective-permute-start(f32[2,4,3,256]{3,2,1,0:T(4,128)S(1)} %get-tuple-element.16), channel_id=1, source_target_pairs={{0,2},{2,4},{4,6},{6,8},{8,10},{10,12},{12,14},{14,16},{16,18},{18... | collective-permute-start | bytes 73736 | tf_op jit(solution)/shard_map/ppermute | solution.py:23
  36.6 32.4 %collective-permute-start = (f32[5,3,8,2048]{3,2,1,0:T(8,128)}, f32[5,3,8,2048]{3,2,1,0:T(8,128)}, u32[]{:S(2)}, u32[]{:S(2)}) collective-permute-start(f32[5,3,8,2048]{3,2,1,0:T(8,128)} %fusion.13), channel_id=1, source_target_pairs={{0,1},{1,0},{2,3},{3,2},{4,5},{5,4},{6,7},{7,6},{8,9},{9,8},{10,11... | collective-permute-start | bytes 2949128 | tf_op jit(solution)/shard_map/ppermute | solution.py:15
  44.5 1.4 copy-start.5
  47.1 0.8 copy-start.4
  47.9 1.3 copy-start.3
  71.5 1.0 copy-start.2
  111.9 20.2 %copy-start = (f32[2,4,67,256]{3,2,1,0:T(8,128)S(1)}, f32[2,4,67,256]{3,2,1,0:T(8,128)}, u32[]{:S(2)}) copy-start(f32[2,4,67,256]{3,2,1,0:T(8,128)} %get-tuple-element.14) | copy-start | bytes 1646596
  111.9 38.1 %all-to-all-start.1 = ((f32[8,1,40960]{2,1,0:T(1,128)}), f32[8,1,40960]{2,1,0:T(1,128)S(1)}, u32[]{:S(2)}, u32[]{:S(2)}) async-start(f32[8,1,40960]{2,1,0:T(1,128)} %reshape.63), calls=%async_computation.1 | async-start | bytes 2621440 | tf_op jit(solution)/shard_map/all_to_all | solution.py:165
